TPU v7x, 32 devices: a whole 2x2x4 slice. The times are simulated.
32 devices in a mesh: gx: 2 (over y), gy: 4 (over z), gz: 4 (over x, core).
Axes of the slice: x: 2, y: 2, z: 4, core: 2. Of those that a mesh axis runs over, the one named last changes fastest.
Arguments:
- right_side: float32 [32, 64, 512], P('gx', 'gy', 'gz'), may hold values from -5 to 5, as said below
- conductivity: float32 [32, 64, 512], P('gx', 'gy', 'gz'), may hold values from 0.1 to 10
Outputs:
- solution: float32 [32, 64, 512], P('gx', 'gy', 'gz')
Inputs may be any that keep to these rules, and one draw needn't show every extreme that they name: `right_side`: a source field of order one.
All inputs are finite; a program needn't handle non-finite values.
Results may differ from a plain program's by a relative error of at most 0.0001.
Values sent between devices are 32-bit elements; how exact they have to be, the bound alone decides.
A program may use at most 64 MiB of HBM per device.

v0:
```python
import functools

import jax
import jax.numpy as jnp
from jax import lax
from jax.experimental import pallas as pl
from jax.experimental.pallas import tpu as pltpu
from jax.sharding import PartitionSpec as P

COARSE = 8
SWEEPS = 4
CSWEEPS = 8
CYCLES = 2
OMEGA = 0.8
LANES = 128
ROWS = 8
DEPTH = SWEEPS + 1
MESH = pl.DeviceIdType.MESH
F32 = jnp.float32
HIGH = lax.Precision.HIGHEST


def kernel(
    counts, block, s_ref, c_ref, o_ref,
    cs, fresh, work_a, work_b, coef, scale, pack_cs, land_cs, pack_v, land_v,
    line, plane, coarse, spread,
    send_sem, recv_sem, line_send, line_recv, plane_send, plane_recv,
):
    nx, ny, nz = counts
    bx, by, bz = block
    px, py = bx + 2 * DEPTH, by + 2 * ROWS
    cx, cy, cz = bx // COARSE, by // COARSE, bz // COARSE
    ypad = line.shape[-2]
    mx, my, mz = lax.axis_index("gx"), lax.axis_index("gy"), lax.axis_index("gz")
    mine = (mx, my, mz)

    def present(offset):
        ok = None
        for here, step, size in zip(mine, offset, counts):
            if step == 0:
                continue
            good = here + step < size if step > 0 else here + step >= 0
            ok = good if ok is None else ok & good
        return ok

    def device(offset):
        return {
            "gx": mx + offset[0], "gy": my + offset[1], "gz": mz + offset[2]
        }

    offsets = [
        (dx, dy, dz)
        for dx in (-1, 0, 1) for dy in (-1, 0, 1) for dz in (-1, 0, 1)
        if (dx, dy, dz) != (0, 0, 0)
        and (dx == 0 or nx > 1) and (dy == 0 or ny > 1) and (dz == 0 or nz > 1)
    ]
    flat = [o for o in offsets if o[2] == 0]
    deep = [o for o in offsets if o[2] != 0]
    number = {o: i for i, o in enumerate(offsets)}

    cs[...] = jnp.zeros_like(cs)
    fresh[...] = jnp.zeros_like(fresh)
    land_cs[...] = jnp.zeros_like(land_cs)
    land_v[...] = jnp.zeros_like(land_v)

    barrier = pltpu.get_barrier_semaphore()
    total = jnp.int32(0)
    for o in offsets:
        ok = present(o)
        total = total + ok.astype(jnp.int32)

        @pl.when(ok)
        def _():
            pl.semaphore_signal(barrier, inc=1, device_id=device(o), device_id_type=MESH)

    for k in range(nz):
        far = jnp.abs(mz - k) >= 2
        total = total + far.astype(jnp.int32)

        @pl.when(far)
        def _():
            pl.semaphore_signal(
                barrier, inc=1, device_id={"gx": mx, "gy": my, "gz": k}, device_id_type=MESH
            )

    for i in range(nx):
        for j in range(ny):
            far = (jnp.abs(mx - i) >= 2) | (jnp.abs(my - j) >= 2)
            total = total + far.astype(jnp.int32)

            @pl.when(far)
            def _():
                pl.semaphore_signal(
                    barrier, inc=1, device_id={"gx": i, "gy": j, "gz": mz}, device_id_type=MESH
                )

    pl.semaphore_wait(barrier, total)

    lane = lax.broadcasted_iota(jnp.int32, (py, LANES), 1)
    lane_by = lax.broadcasted_iota(jnp.int32, (by, LANES), 1)

    xs = {0: pl.ds(DEPTH, bx), 1: pl.ds(bx, DEPTH), -1: pl.ds(DEPTH, DEPTH)}
    xd = {0: pl.ds(DEPTH, bx), 1: pl.ds(0, DEPTH), -1: pl.ds(DEPTH + bx, DEPTH)}
    ys = {0: pl.ds(ROWS, by), 1: pl.ds(by, ROWS), -1: pl.ds(ROWS, ROWS)}
    yd = {0: pl.ds(ROWS, by), 1: pl.ds(0, ROWS), -1: pl.ds(ROWS + by, ROWS)}
    yp = {0: pl.ds(0, by), 1: pl.ds(by - ROWS, ROWS), -1: pl.ds(0, ROWS)}

    def copy(which, o, main, packed, landed):
        dx, dy, dz = o
        if dz == 0:
            source, target = main.at[:, xs[dx], ys[dy]], main.at[:, xd[dx], yd[dy]]
        else:
            side = 0 if dz > 0 else 1
            source = packed.at[side, :, yp[dy]]
            target = landed.at[dx + 1, side, :, yd[dy]]
        return pltpu.make_async_remote_copy(
            src_ref=source, dst_ref=target,
            send_sem=send_sem.at[which, number[o]], recv_sem=recv_sem.at[which, number[o]],
            device_id=device(o), device_id_type=MESH,
        )

    def send_flat(which, main, packed, landed):
        for o in flat:
            @pl.when(present(o))
            def _():
                copy(which, o, main, packed, landed).start()

    def send_deep(which, main, packed, landed):
        for f in range(packed.shape[1]):
            right = jnp.zeros((by, LANES), F32)
            left = jnp.zeros((by, LANES), F32)
            for j in range(bx):
                v = main[f, DEPTH + j, ROWS:ROWS + by]
                here = lane_by // ROWS == j
                right = jnp.where(here, pltpu.roll(v, (ROWS * j + ROWS) % LANES, 1), right)
                left = jnp.where(here, pltpu.roll(v, (ROWS * j) % LANES, 1), left)
            packed[0, f] = right
            packed[1, f] = left
        for o in deep:
            @pl.when(present(o))
            def _():
                copy(which, o, main, packed, landed).start()

    def arrive(which, main, packed, landed):
        for o in flat + deep:
            @pl.when(present(tuple(-step for step in o)))
            def _():
                copy(which, o, main, packed, landed).wait_recv()

    def sent(which, main, packed, landed):
        for o in flat + deep:
            @pl.when(present(o))
            def _():
                copy(which, o, main, packed, landed).wait_send()

    def rim_of(landed, f, x):
        if x < DEPTH:
            slot, j = 2, bx - DEPTH + x
        elif x < DEPTH + bx:
            slot, j = 1, x - DEPTH
        else:
            slot, j = 0, x - DEPTH - bx
        before = pltpu.roll(landed[slot, 0, f], (LANES - ROWS - ROWS * j) % LANES, 1)
        after = pltpu.roll(landed[slot, 1, f], (LANES - ROWS * j) % LANES, 1)
        return jnp.where(
            lane < ROWS, after, jnp.where(lane >= LANES - ROWS, before, 0.0)
        )

    def line_copy(k, p):
        return pltpu.make_async_remote_copy(
            src_ref=line.at[k, mz], dst_ref=line.at[k, mz],
            send_sem=line_send.at[k, p], recv_sem=line_recv.at[k, mz],
            device_id={"gx": mx, "gy": my, "gz": p}, device_id_type=MESH,
        )

    def plane_copy(k, i, j):
        return pltpu.make_async_remote_copy(
            src_ref=plane.at[k, mx, my], dst_ref=plane.at[k, mx, my],
            send_sem=plane_send.at[k, i, j], recv_sem=plane_recv.at[k, mx, my],
            device_id={"gx": i, "gy": j, "gz": mz}, device_id_type=MESH,
        )

    def restrict_send(k, sums):
        row = lax.broadcasted_iota(jnp.int32, (ypad, LANES), 0)
        parts = []
        for a in range(cx):
            out = jnp.zeros((ypad, LANES), F32)
            for b in range(cy):
                t = jnp.sum(sums[a][b * COARSE:(b + 1) * COARSE], axis=0, keepdims=True)
                out = jnp.where(row == my * cy + b, t, out)
            parts.append(out)
        tall = jnp.concatenate(parts, axis=0)
        fine = lax.broadcasted_iota(jnp.int32, (bz, LANES), 0)
        cell = lax.broadcasted_iota(jnp.int32, (bz, LANES), 1)
        place = (cell == mz * cz + fine // COARSE).astype(F32)
        tall = jnp.dot(tall, place, preferred_element_type=F32, precision=HIGH)
        line[k, mz] = tall.reshape(cx, ypad, LANES)
        for p in range(nz):
            @pl.when(p != mz)
            def _():
                line_copy(k, p).start()

    def gather_middle(k):
        for p in range(nz):
            @pl.when(p != mz)
            def _():
                pltpu.make_async_remote_copy(
                    src_ref=line.at[k, p], dst_ref=line.at[k, p],
                    send_sem=line_send.at[k, p], recv_sem=line_recv.at[k, p],
                    device_id={"gx": mx, "gy": my, "gz": p}, device_id_type=MESH,
                ).wait_recv()
        acc = line[k, 0]
        for p in range(1, nz):
            acc = acc + line[k, p]
        plane[k, mx, my] = acc
        for i in range(nx):
            for j in range(ny):
                @pl.when((i != mx) | (j != my))
                def _():
                    plane_copy(k, i, j).start()

    def gather_end(k):
        for i in range(nx):
            for j in range(ny):
                @pl.when((i != mx) | (j != my))
                def _():
                    pltpu.make_async_remote_copy(
                        src_ref=plane.at[k, i, j], dst_ref=plane.at[k, i, j],
                        send_sem=plane_send.at[k, i, j], recv_sem=plane_recv.at[k, i, j],
                        device_id={"gx": i, "gy": j, "gz": mz}, device_id_type=MESH,
                    ).wait_recv()
        parts = []
        for i in range(nx):
            acc = plane[k, i, 0]
            for j in range(1, ny):
                acc = acc + plane[k, i, j]
            parts.append(acc)
        return jnp.concatenate(parts, axis=0)

    def gather_sent(k):
        for p in range(nz):
            @pl.when(p != mz)
            def _():
                line_copy(k, p).wait_send()
        for i in range(nx):
            for j in range(ny):
                @pl.when((i != mx) | (j != my))
                def _():
                    plane_copy(k, i, j).wait_send()

    def six(get, x):
        main, rim = get(0, x), get(1, x)
        m_up, m_down = pltpu.roll(main, 1, 1), pltpu.roll(main, LANES - 1, 1)
        r_up, r_down = pltpu.roll(rim, 1, 1), pltpu.roll(rim, LANES - 1, 1)
        out = []
        for part, v in ((0, main), (1, rim)):
            low = jnp.where(lane == 0, r_up, m_up) if part == 0 else jnp.where(lane == 0, m_up, r_up)
            high = (
                jnp.where(lane == LANES - 1, r_down, m_down) if part == 0
                else jnp.where(lane == LANES - 1, m_down, r_down)
            )
            out.append((v, (
                get(part, x - 1), get(part, x + 1),
                pltpu.roll(v, 1, 0), pltpu.roll(v, py - 1, 0), low, high,
            )))
        return out

    def sweep(source, target, margin):
        def step(x, carry):
            for part, (v, near) in enumerate(six(lambda p, i: source[p, i], x)):
                acc = (1.0 - OMEGA) * v + coef[6, part, x]
                for n in range(6):
                    acc = acc + coef[n, part, x] * near[n]
                target[part, x] = acc
            return carry
        lax.fori_loop(margin, px - margin, step, 0)

    def core(source, x, weight):
        inner = slice(ROWS, ROWS + by)
        v = source[0, x]
        rim = source[1, x, inner]
        mid = v[inner]
        low = jnp.where(lane_by == 0, pltpu.roll(rim, 1, 1), pltpu.roll(mid, 1, 1))
        high = jnp.where(
            lane_by == LANES - 1, pltpu.roll(rim, LANES - 1, 1), pltpu.roll(mid, LANES - 1, 1)
        )
        near = (
            source[0, x - 1, inner], source[0, x + 1, inner],
            pltpu.roll(v, 1, 0)[inner], pltpu.roll(v, py - 1, 0)[inner], low, high,
        )
        acc = weight * mid + coef[6, 0, x, inner]
        for n in range(6):
            acc = acc + coef[n, 0, x, inner] * near[n]
        return acc

    cs[0, 0, DEPTH:DEPTH + bx, ROWS:ROWS + by] = c_ref[...]
    cs[0, 1, DEPTH:DEPTH + bx, ROWS:ROWS + by] = s_ref[...]
    both = cs.at[0]
    send_flat(0, both, pack_cs, land_cs)
    send_deep(0, both, pack_cs, land_cs)

    sums = []
    for a in range(cx):
        acc = c_ref[a * COARSE]
        for t in range(1, COARSE):
            acc = acc + c_ref[a * COARSE + t]
        sums.append(acc * (1.0 / (COARSE * COARSE)))
    restrict_send(0, sums)
    spread[...] = jnp.zeros_like(spread)
    gather_middle(0)
    arrive(0, both, pack_cs, land_cs)

    for f in range(2):
        for x in range(px):
            cs[1, f, x] = rim_of(land_cs, f, x)

    def make(x, carry):
        for part, (c, near) in enumerate(six(lambda p, i: cs[p, 0, i], x)):
            faces = [0.5 * (c + n) for n in near]
            diag = (faces[0] + faces[1]) + (faces[2] + faces[3]) + (faces[4] + faces[5])
            here = c > 0.0
            w = jnp.where(here, OMEGA / jnp.where(here, diag, 1.0), 0.0)
            for n in range(6):
                coef[n, part, x] = w * faces[n]
            first = w * cs[part, 1, x]
            coef[6, part, x] = first
            work_a[part, x] = first
            if part == 0:
                scale[x] = (1.0 / OMEGA) * diag
        return carry
    lax.fori_loop(1, px - 1, make, 0)

    for cycle in range(CYCLES):
        if cycle == 0:
            order, first = [(work_a, work_b), (work_b, work_a), (work_a, work_b)], 2
        else:
            order, first = [(work_a, work_b), (work_b, work_a)] * 2, 1
        for i, (source, target) in enumerate(order):
            sweep(source, target, first + i)
        last = order[-1][1]
        which = 1 + 2 * cycle
        slot = which - 1
        main, packed, landed = fresh.at[slot], pack_v.at[slot], land_v.at[slot]
        fresh[slot, 0, DEPTH:DEPTH + bx, ROWS:ROWS + by] = (
            last[0, DEPTH:DEPTH + bx, ROWS:ROWS + by]
        )

        sums = []
        for a in range(cx):
            def add(t, acc):
                x = DEPTH + a * COARSE + t
                return acc + core(last, x, -OMEGA) * scale[x, ROWS:ROWS + by]
            sums.append(lax.fori_loop(0, COARSE, add, jnp.zeros((by, LANES), F32)))
        restrict_send(1 + cycle, sums)
        send_flat(which, main, packed, landed)
        send_deep(which, main, packed, landed)
        gather_middle(1 + cycle)

        if cycle == 0:
            cc = gather_end(0)
            shape = cc.shape
            row = lax.broadcasted_iota(jnp.int32, shape, 1)
            col = lax.broadcasted_iota(jnp.int32, shape, 2)
            blank = jnp.zeros((1,) + shape[1:], F32)

            def shifts(v):
                return (
                    jnp.concatenate([blank, v[:-1]], axis=0),
                    jnp.concatenate([v[1:], blank], axis=0),
                    jnp.where(row == 0, 0.0, pltpu.roll(v, 1, 1)),
                    jnp.where(row == shape[1] - 1, 0.0, pltpu.roll(v, shape[1] - 1, 1)),
                    jnp.where(col == 0, 0.0, pltpu.roll(v, 1, 2)),
                    jnp.where(col == LANES - 1, 0.0, pltpu.roll(v, LANES - 1, 2)),
                )

            faces = [0.5 * (cc + n) for n in shifts(cc)]
            diag = (faces[0] + faces[1]) + (faces[2] + faces[3]) + (faces[4] + faces[5])
            here = cc > 0.0
            w = jnp.where(here, OMEGA / jnp.where(here, diag, 1.0), 0.0)
            for n in range(6):
                coarse[n] = w * faces[n]
            coarse[6] = w

        rhs = gather_end(1 + cycle) * coarse[6]
        corr = rhs
        for _ in range(CSWEEPS - 1):
            acc = (1.0 - OMEGA) * corr + rhs
            for n, v in enumerate(shifts(corr)):
                acc = acc + coarse[n] * v
            corr = acc

        tall = corr.reshape(-1, LANES)
        cell = lax.broadcasted_iota(jnp.int32, (LANES, LANES), 0)
        fine = lax.broadcasted_iota(jnp.int32, (LANES, LANES), 1)
        to_main = (cell == mz * cz + fine // COARSE).astype(F32)
        to_rim = (
            ((fine < ROWS) & (cell == mz * cz + cz))
            | ((fine >= LANES - ROWS) & (cell == mz * cz - 1))
        ).astype(F32)
        for part, matrix in ((0, to_main), (1, to_rim)):
            wide = jnp.dot(tall, matrix, preferred_element_type=F32, precision=HIGH)
            spread[part, 1:1 + shape[0], ROWS:ROWS + shape[1]] = wide.reshape(shape)

        def lifted(part, x):
            a = mx * cx + 1 + (x - DEPTH) // COARSE
            rows = []
            for t in range(py // ROWS):
                one = spread[part, a, pl.ds(ROWS - 1 + my * cy + t, 1)]
                rows.append(jnp.broadcast_to(one, (ROWS, LANES)))
            return jnp.concatenate(rows, axis=0)

        lifts = {}
        for x in range(px):
            key = (x - DEPTH) // COARSE
            if key not in lifts:
                lifts[key] = (lifted(0, x), lifted(1, x))
        arrive(which, main, packed, landed)
        for x in range(px):
            key = (x - DEPTH) // COARSE
            work_a[0, x] = fresh[slot, 0, x] + lifts[key][0]
            work_a[1, x] = rim_of(land_v.at[slot], 0, x) + lifts[key][1]

        sweep(work_a, work_b, 1)
        sweep(work_b, work_a, 2)
        sweep(work_a, work_b, 3)
        if cycle == CYCLES - 1:
            def finish(x, carry):
                o_ref[x - DEPTH] = core(work_b, x, 1.0 - OMEGA)
                return carry
            lax.fori_loop(DEPTH, DEPTH + bx, finish, 0)
        else:
            which, slot = which + 1, slot + 1
            main, packed, landed = fresh.at[slot], pack_v.at[slot], land_v.at[slot]

            def finish(x, carry):
                fresh[slot, 0, x, ROWS:ROWS + by] = core(work_b, x, 1.0 - OMEGA)
                return carry
            lax.fori_loop(DEPTH, DEPTH + bx, finish, 0)
            send_flat(which, main, packed, landed)
            send_deep(which, main, packed, landed)
            arrive(which, main, packed, landed)
            for x in range(px):
                work_a[0, x] = fresh[slot, 0, x]
                work_a[1, x] = rim_of(land_v.at[slot], 0, x)

    sent(0, both, pack_cs, land_cs)
    for k in range(2 * CYCLES - 1):
        sent(1 + k, fresh.at[k], pack_v.at[k], land_v.at[k])
    for k in range(CYCLES + 1):
        gather_sent(k)


def body(counts, right_side, conductivity):
    nx, ny, nz = counts
    bx, by, bz = block = right_side.shape
    assert bz == LANES and bx * ROWS <= LANES and bx % COARSE == 0 and by % COARSE == 0
    assert nz * bz // COARSE <= LANES
    px, py = bx + 2 * DEPTH, by + 2 * ROWS
    cx = bx // COARSE
    ypad = -(-(ny * by // COARSE) // ROWS) * ROWS
    moves = 2 * CYCLES - 1
    vmem = pltpu.VMEM
    dma = pltpu.SemaphoreType.DMA
    return pl.pallas_call(
        functools.partial(kernel, counts, block),
        out_shape=jax.ShapeDtypeStruct(block, F32),
        in_specs=[pl.BlockSpec(memory_space=vmem)] * 2,
        out_specs=pl.BlockSpec(memory_space=vmem),
        scratch_shapes=[
            vmem((2, 2, px, py, LANES), F32),
            vmem((moves, 1, px, py, LANES), F32),
            vmem((2, px, py, LANES), F32),
            vmem((2, px, py, LANES), F32),
            vmem((7, 2, px, py, LANES), F32),
            vmem((px, py, LANES), F32),
            vmem((2, 2, by, LANES), F32),
            vmem((3, 2, 2, py, LANES), F32),
            vmem((moves, 2, 1, by, LANES), F32),
            vmem((moves, 3, 2, 1, py, LANES), F32),
            vmem((CYCLES + 1, nz, cx, ypad, LANES), F32),
            vmem((CYCLES + 1, nx, ny, cx, ypad, LANES), F32),
            vmem((7, nx * cx, ypad, LANES), F32),
            vmem((2, nx * cx + 2, ypad + 2 * ROWS, LANES), F32),
            dma((moves + 1, 26)),
            dma((moves + 1, 26)),
            dma((CYCLES + 1, nz)),
            dma((CYCLES + 1, nz)),
            dma((CYCLES + 1, nx, ny)),
            dma((CYCLES + 1, nx, ny)),
        ],
        compiler_params=pltpu.CompilerParams(
            collective_id=0, has_side_effects=True, vmem_limit_bytes=40 * 1024 * 1024
        ),
    )(right_side, conductivity)


def solution(mesh):
    counts = tuple(mesh.shape[name] for name in ("gx", "gy", "gz"))
    return jax.shard_map(
        functools.partial(body, counts),
        mesh=mesh,
        in_specs=(P("gx", "gy", "gz"), P("gx", "gy", "gz")),
        out_specs=P("gx", "gy", "gz"),
        check_vma=False,
    )
```

profile of v0, /device:TPU:0, one launch (start us, length us, event | category | flops | bytes accessed | tf_op | source)
XLA Modules:
  0.0 71.9 jit_solution(13406338124752544198)
XLA Ops:
  0.0 0.0 copy-start
  0.0 0.9 %copy-done = f32[16,16,128]{2,1,0:T(8,128)S(1)} copy-done((f32[16,16,128]{2,1,0:T(8,128)S(1)}, f32[16,16,128]{2,1,0:T(8,128)}, u32[]{:S(2)}) %copy-start) | copy-done | bytes 131096
  0.9 0.0 copy-start.1
  0.9 0.9 %copy-done.1 = f32[16,16,128]{2,1,0:T(8,128)S(1)} copy-done((f32[16,16,128]{2,1,0:T(8,128)S(1)}, f32[16,16,128]{2,1,0:T(8,128)}, u32[]{:S(2)}) %copy-start.1) | copy-done | bytes 131096
  1.8 69.5 %shard_map.28 = f32[16,16,128]{2,1,0:T(8,128)S(1)} custom-call(f32[16,16,128]{2,1,0:T(8,128)S(1)} %copy-done, f32[16,16,128]{2,1,0:T(8,128)S(1)} %copy-done.1), custom_call_target="tpu_custom_call" | custom-call | tf_op jit(solution)/shard_map/pallas_call | solution.py:464
  71.3 0.7 copy.4
Async XLA Ops:
  0.0 0.9 %copy-start = (f32[16,16,128]{2,1,0:T(8,128)S(1)}, f32[16,16,128]{2,1,0:T(8,128)}, u32[]{:S(2)}) copy-start(f32[16,16,128]{2,1,0:T(8,128)} %s_ref.1) | copy-start | bytes 393220
  0.9 0.9 %copy-start.1 = (f32[16,16,128]{2,1,0:T(8,128)S(1)}, f32[16,16,128]{2,1,0:T(8,128)}, u32[]{:S(2)}) copy-start(f32[16,16,128]{2,1,0:T(8,128)} %c_ref.1) | copy-start | bytes 393220
where the time goes:
time: 72.1 us; the launch traced here: 71.9 us
  Pallas kernels  69.5 us (96%)
  local copies, waits for them, and re-layouts  2.47 us (3%)
    pallas_call x1, Pallas kernels, body(): pl.pallas_call(functools.partial(kernel, counts, block), out_shape=jax.Sh...  69.5 us
    unnamed x5, local copies, waits for them, and re-layouts  2.47 us

commit v1 on v0

--- a/solution.py
+++ b/solution.py
@@ -24,7 +24,7 @@
     counts, block, s_ref, c_ref, o_ref,
     cs, fresh, work_a, work_b, coef, scale, pack_cs, land_cs, pack_v, land_v,
     line, plane, coarse, spread,
-    send_sem, recv_sem, line_send, line_recv, plane_send, plane_recv,
+    load_sem, send_sem, recv_sem, line_send, line_recv, plane_send, plane_recv,
 ):
     nx, ny, nz = counts
     bx, by, bz = block
@@ -58,7 +58,15 @@
     deep = [o for o in offsets if o[2] != 0]
     number = {o: i for i, o in enumerate(offsets)}
 
-    cs[...] = jnp.zeros_like(cs)
+    cs[0] = jnp.zeros(cs.shape[1:], F32)
+    loads = [
+        pltpu.make_async_copy(
+            ref, cs.at[0, f, pl.ds(DEPTH, bx), pl.ds(2 * ROWS, by)], load_sem.at[f]
+        )
+        for f, ref in ((0, c_ref), (1, s_ref))
+    ]
+    for load in loads:
+        load.start()
     fresh[...] = jnp.zeros_like(fresh)
     land_cs[...] = jnp.zeros_like(land_cs)
     land_v[...] = jnp.zeros_like(land_v)
@@ -94,6 +102,13 @@
                     barrier, inc=1, device_id={"gx": i, "gy": j, "gz": mz}, device_id_type=MESH
                 )
 
+    spread[...] = jnp.zeros_like(spread)
+    for ref in (work_a, work_b, cs.at[1, 0]):
+        lead = ref.shape[:-2]
+        ref[..., 0:ROWS, :] = jnp.zeros(lead + (ROWS, LANES), F32)
+        ref[..., ROWS + py:, :] = jnp.zeros(lead + (ROWS, LANES), F32)
+    for load in loads:
+        load.wait()
     pl.semaphore_wait(barrier, total)
 
     lane = lax.broadcasted_iota(jnp.int32, (py, LANES), 1)
@@ -108,7 +123,9 @@
     def copy(which, o, main, packed, landed):
         dx, dy, dz = o
         if dz == 0:
-            source, target = main.at[:, xs[dx], ys[dy]], main.at[:, xd[dx], yd[dy]]
+            base = 0 if which else ROWS
+            source = main.at[:, xs[dx], pl.ds(ys[dy].start + base, ys[dy].size)]
+            target = main.at[:, xd[dx], pl.ds(yd[dy].start + base, yd[dy].size)]
         else:
             side = 0 if dz > 0 else 1
             source = packed.at[side, :, yp[dy]]
@@ -130,7 +147,8 @@
             right = jnp.zeros((by, LANES), F32)
             left = jnp.zeros((by, LANES), F32)
             for j in range(bx):
-                v = main[f, DEPTH + j, ROWS:ROWS + by]
+                base = ROWS if which else 2 * ROWS
+                v = main[f, DEPTH + j, base:base + by]
                 here = lane_by // ROWS == j
                 right = jnp.where(here, pltpu.roll(v, (ROWS * j + ROWS) % LANES, 1), right)
                 left = jnp.where(here, pltpu.roll(v, (ROWS * j) % LANES, 1), left)
@@ -248,87 +266,99 @@
                 def _():
                     plane_copy(k, i, j).wait_send()
 
-    def six(get, x):
-        main, rim = get(0, x), get(1, x)
-        m_up, m_down = pltpu.roll(main, 1, 1), pltpu.roll(main, LANES - 1, 1)
-        r_up, r_down = pltpu.roll(rim, 1, 1), pltpu.roll(rim, LANES - 1, 1)
+    body_rows = pl.ds(ROWS, py)
+
+    def six(ref, x, size):
+        planes = [[ref[p, x - 1 + i, body_rows] for i in range(size + 2)] for p in (0, 1)]
         out = []
-        for part, v in ((0, main), (1, rim)):
-            low = jnp.where(lane == 0, r_up, m_up) if part == 0 else jnp.where(lane == 0, m_up, r_up)
-            high = (
-                jnp.where(lane == LANES - 1, r_down, m_down) if part == 0
-                else jnp.where(lane == LANES - 1, m_down, r_down)
+        for i in range(1, size + 1):
+            main, rim = planes[0][i], planes[1][i]
+            m_up, m_down = pltpu.roll(main, 1, 1), pltpu.roll(main, LANES - 1, 1)
+            r_up, r_down = pltpu.roll(rim, 1, 1), pltpu.roll(rim, LANES - 1, 1)
+            first, last = lane == 0, lane == LANES - 1
+            ends = (
+                (jnp.where(first, r_up, m_up), jnp.where(last, r_down, m_down)),
+                (jnp.where(first, m_up, r_up), jnp.where(last, m_down, r_down)),
             )
-            out.append((v, (
-                get(part, x - 1), get(part, x + 1),
-                pltpu.roll(v, 1, 0), pltpu.roll(v, py - 1, 0), low, high,
-            )))
+            for p in (0, 1):
+                near = (
+                    planes[p][i - 1], planes[p][i + 1],
+                    ref[p, x - 1 + i, pl.ds(ROWS - 1, py)],
+                    ref[p, x - 1 + i, pl.ds(ROWS + 1, py)],
+                ) + ends[p]
+                out.append((p, x - 1 + i, planes[p][i], near))
         return out
 
+    def group_of(count):
+        return max(g for g in range(1, 12) if count % g == 0)
+
     def sweep(source, target, margin):
-        def step(x, carry):
-            for part, (v, near) in enumerate(six(lambda p, i: source[p, i], x)):
+        count = px - 2 * margin
+        size = group_of(count)
+
+        def step(g, carry):
+            for part, x, v, near in six(source, margin + g * size, size):
                 acc = (1.0 - OMEGA) * v + coef[6, part, x]
                 for n in range(6):
                     acc = acc + coef[n, part, x] * near[n]
-                target[part, x] = acc
+                target[part, x, body_rows] = acc
             return carry
-        lax.fori_loop(margin, px - margin, step, 0)
+        lax.fori_loop(0, count // size, step, 0)
 
     def core(source, x, weight):
-        inner = slice(ROWS, ROWS + by)
-        v = source[0, x]
+        inner = pl.ds(2 * ROWS, by)
+        own = pl.ds(ROWS, by)
+        mid = source[0, x, inner]
         rim = source[1, x, inner]
-        mid = v[inner]
         low = jnp.where(lane_by == 0, pltpu.roll(rim, 1, 1), pltpu.roll(mid, 1, 1))
         high = jnp.where(
             lane_by == LANES - 1, pltpu.roll(rim, LANES - 1, 1), pltpu.roll(mid, LANES - 1, 1)
         )
         near = (
             source[0, x - 1, inner], source[0, x + 1, inner],
-            pltpu.roll(v, 1, 0)[inner], pltpu.roll(v, py - 1, 0)[inner], low, high,
-        )
-        acc = weight * mid + coef[6, 0, x, inner]
+            source[0, x, pl.ds(2 * ROWS - 1, by)], source[0, x, pl.ds(2 * ROWS + 1, by)],
+            low, high,
+        )
+        acc = weight * mid + coef[6, 0, x, own]
         for n in range(6):
-            acc = acc + coef[n, 0, x, inner] * near[n]
+            acc = acc + coef[n, 0, x, own] * near[n]
         return acc
 
-    cs[0, 0, DEPTH:DEPTH + bx, ROWS:ROWS + by] = c_ref[...]
-    cs[0, 1, DEPTH:DEPTH + bx, ROWS:ROWS + by] = s_ref[...]
     both = cs.at[0]
     send_flat(0, both, pack_cs, land_cs)
     send_deep(0, both, pack_cs, land_cs)
 
     sums = []
     for a in range(cx):
-        acc = c_ref[a * COARSE]
-        for t in range(1, COARSE):
-            acc = acc + c_ref[a * COARSE + t]
+        acc = jnp.zeros((by, LANES), F32)
+        for t in range(COARSE):
+            acc = acc + cs[0, 0, DEPTH + a * COARSE + t, 2 * ROWS:2 * ROWS + by]
         sums.append(acc * (1.0 / (COARSE * COARSE)))
     restrict_send(0, sums)
-    spread[...] = jnp.zeros_like(spread)
     gather_middle(0)
     arrive(0, both, pack_cs, land_cs)
 
     for f in range(2):
         for x in range(px):
-            cs[1, f, x] = rim_of(land_cs, f, x)
-
-    def make(x, carry):
-        for part, (c, near) in enumerate(six(lambda p, i: cs[p, 0, i], x)):
+            cs[1, f, x, body_rows] = rim_of(land_cs, f, x)
+
+    size = group_of(px - 2)
+
+    def make(g, carry):
+        for part, x, c, near in six(cs.at[:, 0], 1 + g * size, size):
             faces = [0.5 * (c + n) for n in near]
             diag = (faces[0] + faces[1]) + (faces[2] + faces[3]) + (faces[4] + faces[5])
             here = c > 0.0
             w = jnp.where(here, OMEGA / jnp.where(here, diag, 1.0), 0.0)
             for n in range(6):
                 coef[n, part, x] = w * faces[n]
-            first = w * cs[part, 1, x]
+            first = w * cs[part, 1, x, body_rows]
             coef[6, part, x] = first
-            work_a[part, x] = first
+            work_a[part, x, body_rows] = first
             if part == 0:
                 scale[x] = (1.0 / OMEGA) * diag
         return carry
-    lax.fori_loop(1, px - 1, make, 0)
+    lax.fori_loop(0, (px - 2) // size, make, 0)
 
     for cycle in range(CYCLES):
         if cycle == 0:
@@ -342,15 +372,15 @@
         slot = which - 1
         main, packed, landed = fresh.at[slot], pack_v.at[slot], land_v.at[slot]
         fresh[slot, 0, DEPTH:DEPTH + bx, ROWS:ROWS + by] = (
-            last[0, DEPTH:DEPTH + bx, ROWS:ROWS + by]
+            last[0, DEPTH:DEPTH + bx, 2 * ROWS:2 * ROWS + by]
         )
 
         sums = []
         for a in range(cx):
-            def add(t, acc):
-                x = DEPTH + a * COARSE + t
-                return acc + core(last, x, -OMEGA) * scale[x, ROWS:ROWS + by]
-            sums.append(lax.fori_loop(0, COARSE, add, jnp.zeros((by, LANES), F32)))
+            acc = jnp.zeros((by, LANES), F32)
+            for x in range(DEPTH + a * COARSE, DEPTH + a * COARSE + COARSE):
+                acc = acc + core(last, x, -OMEGA) * scale[x, ROWS:ROWS + by]
+            sums.append(acc)
         restrict_send(1 + cycle, sums)
         send_flat(which, main, packed, landed)
         send_deep(which, main, packed, landed)
@@ -417,31 +447,27 @@
         arrive(which, main, packed, landed)
         for x in range(px):
             key = (x - DEPTH) // COARSE
-            work_a[0, x] = fresh[slot, 0, x] + lifts[key][0]
-            work_a[1, x] = rim_of(land_v.at[slot], 0, x) + lifts[key][1]
+            work_a[0, x, body_rows] = fresh[slot, 0, x] + lifts[key][0]
+            work_a[1, x, body_rows] = rim_of(land_v.at[slot], 0, x) + lifts[key][1]
 
         sweep(work_a, work_b, 1)
         sweep(work_b, work_a, 2)
         sweep(work_a, work_b, 3)
         if cycle == CYCLES - 1:
-            def finish(x, carry):
+            for x in range(DEPTH, DEPTH + bx):
                 o_ref[x - DEPTH] = core(work_b, x, 1.0 - OMEGA)
-                return carry
-            lax.fori_loop(DEPTH, DEPTH + bx, finish, 0)
         else:
             which, slot = which + 1, slot + 1
             main, packed, landed = fresh.at[slot], pack_v.at[slot], land_v.at[slot]
 
-            def finish(x, carry):
+            for x in range(DEPTH, DEPTH + bx):
                 fresh[slot, 0, x, ROWS:ROWS + by] = core(work_b, x, 1.0 - OMEGA)
-                return carry
-            lax.fori_loop(DEPTH, DEPTH + bx, finish, 0)
             send_flat(which, main, packed, landed)
             send_deep(which, main, packed, landed)
             arrive(which, main, packed, landed)
             for x in range(px):
-                work_a[0, x] = fresh[slot, 0, x]
-                work_a[1, x] = rim_of(land_v.at[slot], 0, x)
+                work_a[0, x, body_rows] = fresh[slot, 0, x]
+                work_a[1, x, body_rows] = rim_of(land_v.at[slot], 0, x)
 
     sent(0, both, pack_cs, land_cs)
     for k in range(2 * CYCLES - 1):
@@ -464,13 +490,13 @@
     return pl.pallas_call(
         functools.partial(kernel, counts, block),
         out_shape=jax.ShapeDtypeStruct(block, F32),
-        in_specs=[pl.BlockSpec(memory_space=vmem)] * 2,
+        in_specs=[pl.BlockSpec(memory_space=pltpu.HBM)] * 2,
         out_specs=pl.BlockSpec(memory_space=vmem),
         scratch_shapes=[
-            vmem((2, 2, px, py, LANES), F32),
+            vmem((2, 2, px, py + 2 * ROWS, LANES), F32),
             vmem((moves, 1, px, py, LANES), F32),
-            vmem((2, px, py, LANES), F32),
-            vmem((2, px, py, LANES), F32),
+            vmem((2, px, py + 2 * ROWS, LANES), F32),
+            vmem((2, px, py + 2 * ROWS, LANES), F32),
             vmem((7, 2, px, py, LANES), F32),
             vmem((px, py, LANES), F32),
             vmem((2, 2, by, LANES), F32),
@@ -481,6 +507,7 @@
             vmem((CYCLES + 1, nx, ny, cx, ypad, LANES), F32),
             vmem((7, nx * cx, ypad, LANES), F32),
             vmem((2, nx * cx + 2, ypad + 2 * ROWS, LANES), F32),
+            dma((2,)),
             dma((moves + 1, 26)),
             dma((moves + 1, 26)),
             dma((CYCLES + 1, nz)),

time: 72.1 us -> 49.1 us (0.68)
  Pallas kernels: 69.5 us -> 46.5 us
    pallas_call x1, Pallas kernels: 69.5 us -> 46.5 us  [body(): pl.pallas_call(functools.partial(kernel, counts, block), out_shape=jax.Sh...]
where the time goes in v1:
time: 49.1 us; the launch traced here: 48.9 us
  Pallas kernels  46.5 us (95%)
  local copies, waits for them, and re-layouts  2.47 us (5%)
    pallas_call x1, Pallas kernels, body(): pl.pallas_call(functools.partial(kernel, counts, block), out_shape=jax.Sh...  46.5 us
    unnamed x5, local copies, waits for them, and re-layouts  2.47 us

profile of v1, /device:TPU:0, one launch (start us, length us, event | category | flops | bytes accessed | tf_op | source)
XLA Modules:
  0.0 48.9 jit_solution(10923526294308431153)
XLA Ops:
  0.0 0.0 copy-start
  0.0 0.9 %copy-done = f32[16,16,128]{2,1,0:T(8,128)S(1)} copy-done((f32[16,16,128]{2,1,0:T(8,128)S(1)}, f32[16,16,128]{2,1,0:T(8,128)}, u32[]{:S(2)}) %copy-start) | copy-done | bytes 131096
  0.9 0.0 copy-start.1
  0.9 0.9 %copy-done.1 = f32[16,16,128]{2,1,0:T(8,128)S(1)} copy-done((f32[16,16,128]{2,1,0:T(8,128)S(1)}, f32[16,16,128]{2,1,0:T(8,128)}, u32[]{:S(2)}) %copy-start.1) | copy-done | bytes 131096
  1.8 46.5 %shard_map.28 = f32[16,16,128]{2,1,0:T(8,128)S(1)} custom-call(f32[16,16,128]{2,1,0:T(8,128)S(1)} %copy-done, f32[16,16,128]{2,1,0:T(8,128)S(1)} %copy-done.1), custom_call_target="tpu_custom_call" | custom-call | tf_op jit(solution)/shard_map/pallas_call | solution.py:490
  48.3 0.7 %copy.4 = f32[16,16,128]{2,1,0:T(8,128)} copy(f32[16,16,128]{2,1,0:T(8,128)S(1)} %shard_map.28) | data formatting | bytes 262144
Async XLA Ops:
  0.0 0.9 %copy-start = (f32[16,16,128]{2,1,0:T(8,128)S(1)}, f32[16,16,128]{2,1,0:T(8,128)}, u32[]{:S(2)}) copy-start(f32[16,16,128]{2,1,0:T(8,128)} %s_ref.1) | copy-start | bytes 393220
  0.9 0.9 %copy-start.1 = (f32[16,16,128]{2,1,0:T(8,128)S(1)}, f32[16,16,128]{2,1,0:T(8,128)}, u32[]{:S(2)}) copy-start(f32[16,16,128]{2,1,0:T(8,128)} %c_ref.1) | copy-start | bytes 393220

commit v2 on v1

--- a/solution.py
+++ b/solution.py
@@ -43,20 +43,37 @@
             ok = good if ok is None else ok & good
         return ok
 
+    pair = nx == 2
+    toward = 1 - 2 * mx
+    steps_x = (0, 1) if pair else ((0, 1, -1) if nx > 1 else (0,))
+    steps_y = (0, 1, -1) if ny > 1 else (0,)
+    steps_z = (0, 1, -1) if nz > 1 else (0,)
+    flat_groups = [(dy, 0) for dy in steps_y]
+    deep_groups = [(dy, dz) for dz in steps_z if dz for dy in steps_y]
+    number = {}
+    for dy, dz in flat_groups + deep_groups:
+        for dx in steps_x:
+            if (dx, dy, dz) != (0, 0, 0):
+                number[dx, dy, dz] = len(number)
+
     def device(offset):
-        return {
-            "gx": mx + offset[0], "gy": my + offset[1], "gz": mz + offset[2]
-        }
-
-    offsets = [
-        (dx, dy, dz)
-        for dx in (-1, 0, 1) for dy in (-1, 0, 1) for dz in (-1, 0, 1)
-        if (dx, dy, dz) != (0, 0, 0)
-        and (dx == 0 or nx > 1) and (dy == 0 or ny > 1) and (dz == 0 or nz > 1)
-    ]
-    flat = [o for o in offsets if o[2] == 0]
-    deep = [o for o in offsets if o[2] != 0]
-    number = {o: i for i, o in enumerate(offsets)}
+        dx = toward if pair and offset[0] else offset[0]
+        return {"gx": mx + dx, "gy": my + offset[1], "gz": mz + offset[2]}
+
+    def each(groups, act, sign=1):
+        for dy, dz in groups:
+            def members():
+                for dx in steps_x:
+                    if (dx, dy, dz) not in number:
+                        continue
+                    if dx == 0 or pair:
+                        act((dx, dy, dz))
+                    else:
+                        pl.when(present((sign * dx, 0, 0)))(lambda: act((dx, dy, dz)))
+            if dy == 0 and dz == 0:
+                members()
+            else:
+                pl.when(present((0, sign * dy, sign * dz)))(members)
 
     cs[0] = jnp.zeros(cs.shape[1:], F32)
     loads = [
@@ -73,13 +90,15 @@
 
     barrier = pltpu.get_barrier_semaphore()
     total = jnp.int32(0)
-    for o in offsets:
-        ok = present(o)
-        total = total + ok.astype(jnp.int32)
-
-        @pl.when(ok)
-        def _():
-            pl.semaphore_signal(barrier, inc=1, device_id=device(o), device_id_type=MESH)
+    for o in number:
+        ok = present((0, o[1], o[2]) if pair else o)
+        total = total + (1 if ok is None else ok.astype(jnp.int32))
+    each(
+        flat_groups + deep_groups,
+        lambda o: pl.semaphore_signal(
+            barrier, inc=1, device_id=device(o), device_id_type=MESH
+        ),
+    )
 
     for k in range(nz):
         far = jnp.abs(mz - k) >= 2
@@ -114,22 +133,34 @@
     lane = lax.broadcasted_iota(jnp.int32, (py, LANES), 1)
     lane_by = lax.broadcasted_iota(jnp.int32, (by, LANES), 1)
 
-    xs = {0: pl.ds(DEPTH, bx), 1: pl.ds(bx, DEPTH), -1: pl.ds(DEPTH, DEPTH)}
-    xd = {0: pl.ds(DEPTH, bx), 1: pl.ds(0, DEPTH), -1: pl.ds(DEPTH + bx, DEPTH)}
+    def x_ranges(dx, incoming):
+        if dx == 0:
+            return pl.ds(DEPTH, bx), pl.ds(DEPTH, bx), 1
+        if pair:
+            up = mx if incoming else 1 - mx
+            return (
+                pl.ds(DEPTH + (bx - DEPTH) * up, DEPTH),
+                pl.ds((DEPTH + bx) * (1 - up), DEPTH), 2 * up,
+            )
+        if dx > 0:
+            return pl.ds(bx, DEPTH), pl.ds(0, DEPTH), 2
+        return pl.ds(DEPTH, DEPTH), pl.ds(DEPTH + bx, DEPTH), 0
+
     ys = {0: pl.ds(ROWS, by), 1: pl.ds(by, ROWS), -1: pl.ds(ROWS, ROWS)}
     yd = {0: pl.ds(ROWS, by), 1: pl.ds(0, ROWS), -1: pl.ds(ROWS + by, ROWS)}
     yp = {0: pl.ds(0, by), 1: pl.ds(by - ROWS, ROWS), -1: pl.ds(0, ROWS)}
 
-    def copy(which, o, main, packed, landed):
+    def copy(which, o, main, packed, landed, incoming=False):
         dx, dy, dz = o
+        source_x, target_x, slot = x_ranges(dx, incoming)
         if dz == 0:
             base = 0 if which else ROWS
-            source = main.at[:, xs[dx], pl.ds(ys[dy].start + base, ys[dy].size)]
-            target = main.at[:, xd[dx], pl.ds(yd[dy].start + base, yd[dy].size)]
+            source = main.at[:, source_x, pl.ds(ys[dy].start + base, ys[dy].size)]
+            target = main.at[:, target_x, pl.ds(yd[dy].start + base, yd[dy].size)]
         else:
             side = 0 if dz > 0 else 1
             source = packed.at[side, :, yp[dy]]
-            target = landed.at[dx + 1, side, :, yd[dy]]
+            target = landed.at[slot, side, :, yd[dy]]
         return pltpu.make_async_remote_copy(
             src_ref=source, dst_ref=target,
             send_sem=send_sem.at[which, number[o]], recv_sem=recv_sem.at[which, number[o]],
@@ -137,10 +168,7 @@
         )
 
     def send_flat(which, main, packed, landed):
-        for o in flat:
-            @pl.when(present(o))
-            def _():
-                copy(which, o, main, packed, landed).start()
+        each(flat_groups, lambda o: copy(which, o, main, packed, landed).start())
 
     def send_deep(which, main, packed, landed):
         for f in range(packed.shape[1]):
@@ -154,22 +182,19 @@
                 left = jnp.where(here, pltpu.roll(v, (ROWS * j) % LANES, 1), left)
             packed[0, f] = right
             packed[1, f] = left
-        for o in deep:
-            @pl.when(present(o))
-            def _():
-                copy(which, o, main, packed, landed).start()
+        each(deep_groups, lambda o: copy(which, o, main, packed, landed).start())
 
     def arrive(which, main, packed, landed):
-        for o in flat + deep:
-            @pl.when(present(tuple(-step for step in o)))
-            def _():
-                copy(which, o, main, packed, landed).wait_recv()
+        each(
+            flat_groups + deep_groups,
+            lambda o: copy(which, o, main, packed, landed, True).wait_recv(), -1,
+        )
 
     def sent(which, main, packed, landed):
-        for o in flat + deep:
-            @pl.when(present(o))
-            def _():
-                copy(which, o, main, packed, landed).wait_send()
+        each(
+            flat_groups + deep_groups,
+            lambda o: copy(which, o, main, packed, landed).wait_send(),
+        )
 
     def rim_of(landed, f, x):
         if x < DEPTH:
@@ -184,18 +209,25 @@
             lane < ROWS, after, jnp.where(lane >= LANES - ROWS, before, 0.0)
         )
 
-    def line_copy(k, p):
+    flat_me = mx * ny + my
+
+    def others(me, size):
+        for o in range(1, size):
+            p = me + o
+            yield jnp.where(p >= size, p - size, p)
+
+    def line_copy(k, p, slot):
         return pltpu.make_async_remote_copy(
-            src_ref=line.at[k, mz], dst_ref=line.at[k, mz],
-            send_sem=line_send.at[k, p], recv_sem=line_recv.at[k, mz],
+            src_ref=line.at[k, slot], dst_ref=line.at[k, slot],
+            send_sem=line_send.at[k, p], recv_sem=line_recv.at[k, slot],
             device_id={"gx": mx, "gy": my, "gz": p}, device_id_type=MESH,
         )
 
-    def plane_copy(k, i, j):
+    def plane_copy(k, q, slot):
         return pltpu.make_async_remote_copy(
-            src_ref=plane.at[k, mx, my], dst_ref=plane.at[k, mx, my],
-            send_sem=plane_send.at[k, i, j], recv_sem=plane_recv.at[k, mx, my],
-            device_id={"gx": i, "gy": j, "gz": mz}, device_id_type=MESH,
+            src_ref=plane.at[k, slot], dst_ref=plane.at[k, slot],
+            send_sem=plane_send.at[k, q], recv_sem=plane_recv.at[k, slot],
+            device_id={"gx": q // ny, "gy": q % ny, "gz": mz}, device_id_type=MESH,
         )
 
     def restrict_send(k, sums):
@@ -213,58 +245,37 @@
         place = (cell == mz * cz + fine // COARSE).astype(F32)
         tall = jnp.dot(tall, place, preferred_element_type=F32, precision=HIGH)
         line[k, mz] = tall.reshape(cx, ypad, LANES)
-        for p in range(nz):
-            @pl.when(p != mz)
-            def _():
-                line_copy(k, p).start()
+        for p in others(mz, nz):
+            line_copy(k, p, mz).start()
 
     def gather_middle(k):
-        for p in range(nz):
-            @pl.when(p != mz)
-            def _():
-                pltpu.make_async_remote_copy(
-                    src_ref=line.at[k, p], dst_ref=line.at[k, p],
-                    send_sem=line_send.at[k, p], recv_sem=line_recv.at[k, p],
-                    device_id={"gx": mx, "gy": my, "gz": p}, device_id_type=MESH,
-                ).wait_recv()
+        for p in others(mz, nz):
+            line_copy(k, p, p).wait_recv()
         acc = line[k, 0]
         for p in range(1, nz):
             acc = acc + line[k, p]
-        plane[k, mx, my] = acc
-        for i in range(nx):
-            for j in range(ny):
-                @pl.when((i != mx) | (j != my))
-                def _():
-                    plane_copy(k, i, j).start()
+        plane[k, flat_me] = acc
+        for q in others(flat_me, nx * ny):
+            plane_copy(k, q, flat_me).start()
 
     def gather_end(k):
-        for i in range(nx):
-            for j in range(ny):
-                @pl.when((i != mx) | (j != my))
-                def _():
-                    pltpu.make_async_remote_copy(
-                        src_ref=plane.at[k, i, j], dst_ref=plane.at[k, i, j],
-                        send_sem=plane_send.at[k, i, j], recv_sem=plane_recv.at[k, i, j],
-                        device_id={"gx": i, "gy": j, "gz": mz}, device_id_type=MESH,
-                    ).wait_recv()
+        for q in others(flat_me, nx * ny):
+            plane_copy(k, q, q).wait_recv()
         parts = []
         for i in range(nx):
-            acc = plane[k, i, 0]
+            acc = plane[k, i * ny]
             for j in range(1, ny):
-                acc = acc + plane[k, i, j]
+                acc = acc + plane[k, i * ny + j]
             parts.append(acc)
         return jnp.concatenate(parts, axis=0)
 
-    def gather_sent(k):
-        for p in range(nz):
-            @pl.when(p != mz)
-            def _():
-                line_copy(k, p).wait_send()
-        for i in range(nx):
-            for j in range(ny):
-                @pl.when((i != mx) | (j != my))
-                def _():
-                    plane_copy(k, i, j).wait_send()
+    def line_sent(k):
+        for p in others(mz, nz):
+            line_copy(k, p, mz).wait_send()
+
+    def plane_sent(k):
+        for q in others(flat_me, nx * ny):
+            plane_copy(k, q, flat_me).wait_send()
 
     body_rows = pl.ds(ROWS, py)
 
@@ -386,6 +397,18 @@
         send_deep(which, main, packed, landed)
         gather_middle(1 + cycle)
 
+        line_sent(1 + cycle)
+        if cycle == 0:
+            sent(0, both, pack_cs, land_cs)
+            line_sent(0)
+            plane_sent(0)
+        else:
+            plane_sent(cycle)
+        sent(which, main, packed, landed)
+        arrive(which, main, packed, landed)
+        for x in range(px):
+            work_a[1, x, body_rows] = rim_of(land_v.at[slot], 0, x)
+
         if cycle == 0:
             cc = gather_end(0)
             shape = cc.shape
@@ -444,11 +467,10 @@
             key = (x - DEPTH) // COARSE
             if key not in lifts:
                 lifts[key] = (lifted(0, x), lifted(1, x))
-        arrive(which, main, packed, landed)
         for x in range(px):
             key = (x - DEPTH) // COARSE
             work_a[0, x, body_rows] = fresh[slot, 0, x] + lifts[key][0]
-            work_a[1, x, body_rows] = rim_of(land_v.at[slot], 0, x) + lifts[key][1]
+            work_a[1, x, body_rows] = work_a[1, x, body_rows] + lifts[key][1]
 
         sweep(work_a, work_b, 1)
         sweep(work_b, work_a, 2)
@@ -464,16 +486,13 @@
                 fresh[slot, 0, x, ROWS:ROWS + by] = core(work_b, x, 1.0 - OMEGA)
             send_flat(which, main, packed, landed)
             send_deep(which, main, packed, landed)
+            sent(which, main, packed, landed)
             arrive(which, main, packed, landed)
             for x in range(px):
                 work_a[0, x, body_rows] = fresh[slot, 0, x]
                 work_a[1, x, body_rows] = rim_of(land_v.at[slot], 0, x)
 
-    sent(0, both, pack_cs, land_cs)
-    for k in range(2 * CYCLES - 1):
-        sent(1 + k, fresh.at[k], pack_v.at[k], land_v.at[k])
-    for k in range(CYCLES + 1):
-        gather_sent(k)
+    plane_sent(CYCLES)
 
 
 def body(counts, right_side, conductivity):
@@ -504,7 +523,7 @@
             vmem((moves, 2, 1, by, LANES), F32),
             vmem((moves, 3, 2, 1, py, LANES), F32),
             vmem((CYCLES + 1, nz, cx, ypad, LANES), F32),
-            vmem((CYCLES + 1, nx, ny, cx, ypad, LANES), F32),
+            vmem((CYCLES + 1, nx * ny, cx, ypad, LANES), F32),
             vmem((7, nx * cx, ypad, LANES), F32),
             vmem((2, nx * cx + 2, ypad + 2 * ROWS, LANES), F32),
             dma((2,)),
@@ -512,11 +531,11 @@
             dma((moves + 1, 26)),
             dma((CYCLES + 1, nz)),
             dma((CYCLES + 1, nz)),
-            dma((CYCLES + 1, nx, ny)),
-            dma((CYCLES + 1, nx, ny)),
+            dma((CYCLES + 1, nx * ny)),
+            dma((CYCLES + 1, nx * ny)),
         ],
         compiler_params=pltpu.CompilerParams(
-            collective_id=0, has_side_effects=True, vmem_limit_bytes=40 * 1024 * 1024
+            collective_id=0, has_side_effects=True, vmem_limit_bytes=60 * 1024 * 1024
         ),
     )(right_side, conductivity)
 

time: 49.1 us -> 48.2 us (0.982)
  local copies, waits for them, and re-layouts: 2.47 us -> 1.57 us
    unnamed x5 -> x1, local copies, waits for them, and re-layouts: 2.47 us -> 1.57 us
where the time goes in v2:
time: 48.2 us; the launch traced here: 48 us
  Pallas kernels  46.5 us (96%)
  local copies, waits for them, and re-layouts  1.57 us (3%)
    pallas_call x1, Pallas kernels, body(): pl.pallas_call(functools.partial(kernel, counts, block), out_shape=jax.Sh...  46.5 us
    unnamed x1, local copies, waits for them, and re-layouts  1.57 us

profile of v2, /device:TPU:0, one launch (start us, length us, event | category | flops | bytes accessed | tf_op | source)
XLA Modules:
  0.0 48.0 jit_solution(10494454010357516370)
XLA Ops:
  0.0 46.5 %shard_map.28 = f32[16,16,128]{2,1,0:T(8,128)} custom-call(f32[16,16,128]{2,1,0:T(8,128)} %s_ref.1, f32[16,16,128]{2,1,0:T(8,128)} %c_ref.1), custom_call_target="tpu_custom_call" | custom-call | tf_op jit(solution)/shard_map/pallas_call | solution.py:509
  46.5 1.6 %copy.4 = f32[16,16,128]{2,1,0:T(8,128)} copy(f32[16,16,128]{2,1,0:T(8,128)} %shard_map.28) | data formatting | bytes 262144

commit v3 on v2

--- a/solution.py
+++ b/solution.py
@@ -22,7 +22,7 @@
 
 def kernel(
     counts, block, s_ref, c_ref, o_ref,
-    cs, fresh, work_a, work_b, coef, scale, pack_cs, land_cs, pack_v, land_v,
+    cs, fresh, work_a, work_b, rim_a, rim_b, coef, rim_coef, scale, pack_cs, land_cs, pack_v, land_v,
     line, plane, coarse, spread,
     load_sem, send_sem, recv_sem, line_send, line_recv, plane_send, plane_recv,
 ):
@@ -75,10 +75,10 @@
             else:
                 pl.when(present((0, sign * dy, sign * dz)))(members)
 
-    cs[0] = jnp.zeros(cs.shape[1:], F32)
+    cs[...] = jnp.zeros_like(cs)
     loads = [
         pltpu.make_async_copy(
-            ref, cs.at[0, f, pl.ds(DEPTH, bx), pl.ds(2 * ROWS, by)], load_sem.at[f]
+            ref, cs.at[f, pl.ds(DEPTH, bx), pl.ds(2 * ROWS, by)], load_sem.at[f]
         )
         for f, ref in ((0, c_ref), (1, s_ref))
     ]
@@ -122,7 +122,7 @@
                 )
 
     spread[...] = jnp.zeros_like(spread)
-    for ref in (work_a, work_b, cs.at[1, 0]):
+    for ref in (work_a, work_b, rim_a, rim_b):
         lead = ref.shape[:-2]
         ref[..., 0:ROWS, :] = jnp.zeros(lead + (ROWS, LANES), F32)
         ref[..., ROWS + py:, :] = jnp.zeros(lead + (ROWS, LANES), F32)
@@ -140,23 +140,22 @@
             up = mx if incoming else 1 - mx
             return (
                 pl.ds(DEPTH + (bx - DEPTH) * up, DEPTH),
-                pl.ds((DEPTH + bx) * (1 - up), DEPTH), 2 * up,
+                pl.ds((DEPTH + bx) * (1 - up), DEPTH), 2 * (1 - up),
             )
         if dx > 0:
-            return pl.ds(bx, DEPTH), pl.ds(0, DEPTH), 2
-        return pl.ds(DEPTH, DEPTH), pl.ds(DEPTH + bx, DEPTH), 0
-
-    ys = {0: pl.ds(ROWS, by), 1: pl.ds(by, ROWS), -1: pl.ds(ROWS, ROWS)}
-    yd = {0: pl.ds(ROWS, by), 1: pl.ds(0, ROWS), -1: pl.ds(ROWS + by, ROWS)}
+            return pl.ds(bx, DEPTH), pl.ds(0, DEPTH), 0
+        return pl.ds(DEPTH, DEPTH), pl.ds(DEPTH + bx, DEPTH), 2
+
+    ys = {0: pl.ds(2 * ROWS, by), 1: pl.ds(ROWS + by, ROWS), -1: pl.ds(2 * ROWS, ROWS)}
+    yd = {0: pl.ds(2 * ROWS, by), 1: pl.ds(ROWS, ROWS), -1: pl.ds(2 * ROWS + by, ROWS)}
     yp = {0: pl.ds(0, by), 1: pl.ds(by - ROWS, ROWS), -1: pl.ds(0, ROWS)}
 
     def copy(which, o, main, packed, landed, incoming=False):
         dx, dy, dz = o
         source_x, target_x, slot = x_ranges(dx, incoming)
         if dz == 0:
-            base = 0 if which else ROWS
-            source = main.at[:, source_x, pl.ds(ys[dy].start + base, ys[dy].size)]
-            target = main.at[:, target_x, pl.ds(yd[dy].start + base, yd[dy].size)]
+            source = main.at[:, source_x, ys[dy]]
+            target = main.at[:, target_x, yd[dy]]
         else:
             side = 0 if dz > 0 else 1
             source = packed.at[side, :, yp[dy]]
@@ -175,8 +174,7 @@
             right = jnp.zeros((by, LANES), F32)
             left = jnp.zeros((by, LANES), F32)
             for j in range(bx):
-                base = ROWS if which else 2 * ROWS
-                v = main[f, DEPTH + j, base:base + by]
+                v = main[f, DEPTH + j, 2 * ROWS:2 * ROWS + by]
                 here = lane_by // ROWS == j
                 right = jnp.where(here, pltpu.roll(v, (ROWS * j + ROWS) % LANES, 1), right)
                 left = jnp.where(here, pltpu.roll(v, (ROWS * j) % LANES, 1), left)
@@ -194,19 +192,6 @@
         each(
             flat_groups + deep_groups,
             lambda o: copy(which, o, main, packed, landed).wait_send(),
-        )
-
-    def rim_of(landed, f, x):
-        if x < DEPTH:
-            slot, j = 2, bx - DEPTH + x
-        elif x < DEPTH + bx:
-            slot, j = 1, x - DEPTH
-        else:
-            slot, j = 0, x - DEPTH - bx
-        before = pltpu.roll(landed[slot, 0, f], (LANES - ROWS - ROWS * j) % LANES, 1)
-        after = pltpu.roll(landed[slot, 1, f], (LANES - ROWS * j) % LANES, 1)
-        return jnp.where(
-            lane < ROWS, after, jnp.where(lane >= LANES - ROWS, before, 0.0)
         )
 
     flat_me = mx * ny + my
@@ -278,64 +263,92 @@
             plane_copy(k, q, flat_me).wait_send()
 
     body_rows = pl.ds(ROWS, py)
-
-    def six(ref, x, size):
-        planes = [[ref[p, x - 1 + i, body_rows] for i in range(size + 2)] for p in (0, 1)]
-        out = []
-        for i in range(1, size + 1):
-            main, rim = planes[0][i], planes[1][i]
-            m_up, m_down = pltpu.roll(main, 1, 1), pltpu.roll(main, LANES - 1, 1)
-            r_up, r_down = pltpu.roll(rim, 1, 1), pltpu.roll(rim, LANES - 1, 1)
-            first, last = lane == 0, lane == LANES - 1
-            ends = (
-                (jnp.where(first, r_up, m_up), jnp.where(last, r_down, m_down)),
-                (jnp.where(first, m_up, r_up), jnp.where(last, m_down, r_down)),
+    own_rows = pl.ds(2 * ROWS, by)
+    sides = [(slot, side) for slot in range(3) for side in range(2)]
+
+    def lanes(rows):
+        return lax.broadcasted_iota(jnp.int32, (rows.size, LANES), 1)
+
+    def place_of(x):
+        if x < DEPTH:
+            return 0, bx - DEPTH + x
+        if x < DEPTH + bx:
+            return 1, x - DEPTH
+        return 2, x - DEPTH - bx
+
+    def ends_of(rim, rows):
+        last = lanes(rows) % ROWS == ROWS - 1
+        return [
+            jnp.where(last, rim[slot, 0, rows], pltpu.roll(rim[slot, 1, rows], ROWS - 2, 1))
+            for slot in range(3)
+        ]
+
+    def near_main(main, ends, x, rows):
+        lane = lanes(rows)
+        slot, j = place_of(x)
+        v = main[x, rows]
+        up, down = pltpu.roll(v, 1, 1), pltpu.roll(v, LANES - 1, 1)
+        end = pltpu.roll(ends[slot], (2 * LANES - ROWS * j - ROWS + 1) % LANES, 1)
+        return v, up, (
+            main[x - 1, rows], main[x + 1, rows],
+            main[x, pl.ds(rows.start - 1, rows.size)], main[x, pl.ds(rows.start + 1, rows.size)],
+            jnp.where(lane == 0, end, up), jnp.where(lane == LANES - 1, end, down),
+        )
+
+    def collect(tips, x, up):
+        slot, j = place_of(x)
+        turned = pltpu.roll(up, ROWS * j, 1) if j else up
+        tips[slot] = jnp.where(lane // ROWS == j, turned, tips[slot])
+
+    def near_rim(rim, tips, slot, side):
+        rows = body_rows
+        q = rim[slot, side, rows]
+        zero = jnp.zeros((py, LANES), F32)
+        before = pltpu.roll(rim[slot - 1, side, rows], ROWS, 1) if slot > 0 else zero
+        after = pltpu.roll(rim[slot + 1, side, rows], LANES - ROWS, 1) if slot < 2 else zero
+        low, high = pltpu.roll(q, 1, 1), pltpu.roll(q, LANES - 1, 1)
+        if side == 0:
+            high = jnp.where(
+                lane % ROWS == ROWS - 1, pltpu.roll(tips[slot], ROWS - 2, 1), high
             )
-            for p in (0, 1):
-                near = (
-                    planes[p][i - 1], planes[p][i + 1],
-                    ref[p, x - 1 + i, pl.ds(ROWS - 1, py)],
-                    ref[p, x - 1 + i, pl.ds(ROWS + 1, py)],
-                ) + ends[p]
-                out.append((p, x - 1 + i, planes[p][i], near))
-        return out
-
-    def group_of(count):
-        return max(g for g in range(1, 12) if count % g == 0)
+        else:
+            low = jnp.where(lane % ROWS == 0, tips[slot], low)
+        return q, (
+            jnp.where(lane < ROWS, before, pltpu.roll(q, ROWS, 1)),
+            jnp.where(lane >= LANES - ROWS, after, pltpu.roll(q, LANES - ROWS, 1)),
+            rim[slot, side, pl.ds(ROWS - 1, py)], rim[slot, side, pl.ds(ROWS + 1, py)],
+            low, high,
+        )
+
+    def no_tips():
+        return [jnp.zeros((py, LANES), F32) for _ in range(3)]
 
     def sweep(source, target, margin):
-        count = px - 2 * margin
-        size = group_of(count)
-
-        def step(g, carry):
-            for part, x, v, near in six(source, margin + g * size, size):
-                acc = (1.0 - OMEGA) * v + coef[6, part, x]
-                for n in range(6):
-                    acc = acc + coef[n, part, x] * near[n]
-                target[part, x, body_rows] = acc
-            return carry
-        lax.fori_loop(0, count // size, step, 0)
-
-    def core(source, x, weight):
-        inner = pl.ds(2 * ROWS, by)
+        main, rim = source
+        ends, tips = ends_of(rim, body_rows), no_tips()
+        for x in range(margin, px - margin):
+            v, up, near = near_main(main, ends, x, body_rows)
+            collect(tips, x, up)
+            acc = (1.0 - OMEGA) * v + coef[6, x]
+            for n in range(6):
+                acc = acc + coef[n, x] * near[n]
+            target[0][x, body_rows] = acc
+        for slot, side in sides:
+            q, near = near_rim(rim, tips, slot, side)
+            acc = (1.0 - OMEGA) * q + rim_coef[6, slot, side]
+            for n in range(6):
+                acc = acc + rim_coef[n, slot, side] * near[n]
+            target[1][slot, side, body_rows] = acc
+
+    def core(source, x, ends, weight):
+        v, _, near = near_main(source[0], ends, x, own_rows)
         own = pl.ds(ROWS, by)
-        mid = source[0, x, inner]
-        rim = source[1, x, inner]
-        low = jnp.where(lane_by == 0, pltpu.roll(rim, 1, 1), pltpu.roll(mid, 1, 1))
-        high = jnp.where(
-            lane_by == LANES - 1, pltpu.roll(rim, LANES - 1, 1), pltpu.roll(mid, LANES - 1, 1)
-        )
-        near = (
-            source[0, x - 1, inner], source[0, x + 1, inner],
-            source[0, x, pl.ds(2 * ROWS - 1, by)], source[0, x, pl.ds(2 * ROWS + 1, by)],
-            low, high,
-        )
-        acc = weight * mid + coef[6, 0, x, own]
+        acc = weight * v + coef[6, x, own]
         for n in range(6):
-            acc = acc + coef[n, 0, x, own] * near[n]
+            acc = acc + coef[n, x, own] * near[n]
         return acc
 
-    both = cs.at[0]
+    both = cs
     send_flat(0, both, pack_cs, land_cs)
     send_deep(0, both, pack_cs, land_cs)
 
@@ -343,54 +356,63 @@
     for a in range(cx):
         acc = jnp.zeros((by, LANES), F32)
         for t in range(COARSE):
-            acc = acc + cs[0, 0, DEPTH + a * COARSE + t, 2 * ROWS:2 * ROWS + by]
+            acc = acc + cs[0, DEPTH + a * COARSE + t, 2 * ROWS:2 * ROWS + by]
         sums.append(acc * (1.0 / (COARSE * COARSE)))
     restrict_send(0, sums)
     gather_middle(0)
     arrive(0, both, pack_cs, land_cs)
 
-    for f in range(2):
-        for x in range(px):
-            cs[1, f, x, body_rows] = rim_of(land_cs, f, x)
-
-    size = group_of(px - 2)
-
-    def make(g, carry):
-        for part, x, c, near in six(cs.at[:, 0], 1 + g * size, size):
-            faces = [0.5 * (c + n) for n in near]
-            diag = (faces[0] + faces[1]) + (faces[2] + faces[3]) + (faces[4] + faces[5])
-            here = c > 0.0
-            w = jnp.where(here, OMEGA / jnp.where(here, diag, 1.0), 0.0)
-            for n in range(6):
-                coef[n, part, x] = w * faces[n]
-            first = w * cs[part, 1, x, body_rows]
-            coef[6, part, x] = first
-            work_a[part, x, body_rows] = first
-            if part == 0:
-                scale[x] = (1.0 / OMEGA) * diag
-        return carry
-    lax.fori_loop(0, (px - 2) // size, make, 0)
-
+    def weights(c, near):
+        faces = [0.5 * (c + n) for n in near]
+        diag = (faces[0] + faces[1]) + (faces[2] + faces[3]) + (faces[4] + faces[5])
+        here = c > 0.0
+        w = jnp.where(here, OMEGA / jnp.where(here, diag, 1.0), 0.0)
+        return faces, diag, w
+
+    rim_c = land_cs.at[:, :, 0]
+    ends, tips = ends_of(rim_c, body_rows), no_tips()
+    for x in range(1, px - 1):
+        c, up, near = near_main(cs.at[0], ends, x, body_rows)
+        collect(tips, x, up)
+        faces, diag, w = weights(c, near)
+        for n in range(6):
+            coef[n, x] = w * faces[n]
+        first = w * cs[1, x, body_rows]
+        coef[6, x] = first
+        work_a[x, body_rows] = first
+        scale[x] = (1.0 / OMEGA) * diag
+    for slot, side in sides:
+        c, near = near_rim(rim_c, tips, slot, side)
+        faces, diag, w = weights(c, near)
+        for n in range(6):
+            rim_coef[n, slot, side] = w * faces[n]
+        first = w * land_cs[slot, side, 1, body_rows]
+        rim_coef[6, slot, side] = first
+        rim_a[slot, side, body_rows] = first
+
+    field_a, field_b = (work_a, rim_a), (work_b, rim_b)
     for cycle in range(CYCLES):
         if cycle == 0:
-            order, first = [(work_a, work_b), (work_b, work_a), (work_a, work_b)], 2
+            order, first = [(field_a, field_b), (field_b, field_a), (field_a, field_b)], 2
         else:
-            order, first = [(work_a, work_b), (work_b, work_a)] * 2, 1
+            order = [(start, field_b), (field_b, field_a), (field_a, field_b), (field_b, field_a)]
+            first = 1
         for i, (source, target) in enumerate(order):
             sweep(source, target, first + i)
         last = order[-1][1]
         which = 1 + 2 * cycle
         slot = which - 1
         main, packed, landed = fresh.at[slot], pack_v.at[slot], land_v.at[slot]
-        fresh[slot, 0, DEPTH:DEPTH + bx, ROWS:ROWS + by] = (
-            last[0, DEPTH:DEPTH + bx, 2 * ROWS:2 * ROWS + by]
+        fresh[slot, 0, DEPTH:DEPTH + bx, 2 * ROWS:2 * ROWS + by] = (
+            last[0][DEPTH:DEPTH + bx, 2 * ROWS:2 * ROWS + by]
         )
 
         sums = []
+        ends = ends_of(last[1], own_rows)
         for a in range(cx):
             acc = jnp.zeros((by, LANES), F32)
             for x in range(DEPTH + a * COARSE, DEPTH + a * COARSE + COARSE):
-                acc = acc + core(last, x, -OMEGA) * scale[x, ROWS:ROWS + by]
+                acc = acc + core(last, x, ends, -OMEGA) * scale[x, ROWS:ROWS + by]
             sums.append(acc)
         restrict_send(1 + cycle, sums)
         send_flat(which, main, packed, landed)
@@ -406,8 +428,6 @@
             plane_sent(cycle)
         sent(which, main, packed, landed)
         arrive(which, main, packed, landed)
-        for x in range(px):
-            work_a[1, x, body_rows] = rim_of(land_v.at[slot], 0, x)
 
         if cycle == 0:
             cc = gather_end(0)
@@ -446,51 +466,48 @@
         cell = lax.broadcasted_iota(jnp.int32, (LANES, LANES), 0)
         fine = lax.broadcasted_iota(jnp.int32, (LANES, LANES), 1)
         to_main = (cell == mz * cz + fine // COARSE).astype(F32)
-        to_rim = (
-            ((fine < ROWS) & (cell == mz * cz + cz))
-            | ((fine >= LANES - ROWS) & (cell == mz * cz - 1))
-        ).astype(F32)
-        for part, matrix in ((0, to_main), (1, to_rim)):
+        to_left = (cell == mz * cz - 1).astype(F32)
+        to_right = (cell == mz * cz + cz).astype(F32)
+        for part, matrix in enumerate((to_main, to_left, to_right)):
             wide = jnp.dot(tall, matrix, preferred_element_type=F32, precision=HIGH)
             spread[part, 1:1 + shape[0], ROWS:ROWS + shape[1]] = wide.reshape(shape)
 
-        def lifted(part, x):
-            a = mx * cx + 1 + (x - DEPTH) // COARSE
+        def lifted(part, a):
             rows = []
             for t in range(py // ROWS):
-                one = spread[part, a, pl.ds(ROWS - 1 + my * cy + t, 1)]
+                one = spread[part, mx * cx + 1 + a, pl.ds(ROWS - 1 + my * cy + t, 1)]
                 rows.append(jnp.broadcast_to(one, (ROWS, LANES)))
             return jnp.concatenate(rows, axis=0)
 
-        lifts = {}
+        lifts = [lifted(0, a) for a in range(-1, cx + 1)]
         for x in range(px):
-            key = (x - DEPTH) // COARSE
-            if key not in lifts:
-                lifts[key] = (lifted(0, x), lifted(1, x))
-        for x in range(px):
-            key = (x - DEPTH) // COARSE
-            work_a[0, x, body_rows] = fresh[slot, 0, x] + lifts[key][0]
-            work_a[1, x, body_rows] = work_a[1, x, body_rows] + lifts[key][1]
-
-        sweep(work_a, work_b, 1)
-        sweep(work_b, work_a, 2)
-        sweep(work_a, work_b, 3)
+            work_a[x, body_rows] = (
+                fresh[slot, 0, x, body_rows] + lifts[(x - DEPTH) // COARSE + 1]
+            )
+        for side in range(2):
+            own = lifted(1 + side, 0)
+            for a in range(1, cx):
+                own = jnp.where(lane // (COARSE * ROWS) == a, lifted(1 + side, a), own)
+            for k, lift in enumerate((lifted(1 + side, -1), own, lifted(1 + side, cx))):
+                rim_a[k, side, body_rows] = land_v[slot, k, side, 0, body_rows] + lift
+
+        sweep(field_a, field_b, 1)
+        sweep(field_b, field_a, 2)
+        sweep(field_a, field_b, 3)
+        ends = ends_of(rim_b, own_rows)
         if cycle == CYCLES - 1:
             for x in range(DEPTH, DEPTH + bx):
-                o_ref[x - DEPTH] = core(work_b, x, 1.0 - OMEGA)
+                o_ref[x - DEPTH] = core(field_b, x, ends, 1.0 - OMEGA)
         else:
             which, slot = which + 1, slot + 1
             main, packed, landed = fresh.at[slot], pack_v.at[slot], land_v.at[slot]
-
             for x in range(DEPTH, DEPTH + bx):
-                fresh[slot, 0, x, ROWS:ROWS + by] = core(work_b, x, 1.0 - OMEGA)
+                fresh[slot, 0, x, 2 * ROWS:2 * ROWS + by] = core(field_b, x, ends, 1.0 - OMEGA)
             send_flat(which, main, packed, landed)
             send_deep(which, main, packed, landed)
             sent(which, main, packed, landed)
             arrive(which, main, packed, landed)
-            for x in range(px):
-                work_a[0, x, body_rows] = fresh[slot, 0, x]
-                work_a[1, x, body_rows] = rim_of(land_v.at[slot], 0, x)
+            start = (fresh.at[slot, 0], land_v.at[slot, :, :, 0])
 
     plane_sent(CYCLES)
 
@@ -498,9 +515,10 @@
 def body(counts, right_side, conductivity):
     nx, ny, nz = counts
     bx, by, bz = block = right_side.shape
-    assert bz == LANES and bx * ROWS <= LANES and bx % COARSE == 0 and by % COARSE == 0
+    assert bz == LANES and bx * ROWS == LANES and COARSE == ROWS and bx % COARSE == 0 and by % COARSE == 0
     assert nz * bz // COARSE <= LANES
     px, py = bx + 2 * DEPTH, by + 2 * ROWS
+    tall = py + 2 * ROWS
     cx = bx // COARSE
     ypad = -(-(ny * by // COARSE) // ROWS) * ROWS
     moves = 2 * CYCLES - 1
@@ -512,20 +530,23 @@
         in_specs=[pl.BlockSpec(memory_space=pltpu.HBM)] * 2,
         out_specs=pl.BlockSpec(memory_space=vmem),
         scratch_shapes=[
-            vmem((2, 2, px, py + 2 * ROWS, LANES), F32),
-            vmem((moves, 1, px, py, LANES), F32),
-            vmem((2, px, py + 2 * ROWS, LANES), F32),
-            vmem((2, px, py + 2 * ROWS, LANES), F32),
-            vmem((7, 2, px, py, LANES), F32),
+            vmem((2, px, tall, LANES), F32),
+            vmem((moves, 1, px, tall, LANES), F32),
+            vmem((px, tall, LANES), F32),
+            vmem((px, tall, LANES), F32),
+            vmem((3, 2, tall, LANES), F32),
+            vmem((3, 2, tall, LANES), F32),
+            vmem((7, px, py, LANES), F32),
+            vmem((7, 3, 2, py, LANES), F32),
             vmem((px, py, LANES), F32),
             vmem((2, 2, by, LANES), F32),
-            vmem((3, 2, 2, py, LANES), F32),
+            vmem((3, 2, 2, tall, LANES), F32),
             vmem((moves, 2, 1, by, LANES), F32),
-            vmem((moves, 3, 2, 1, py, LANES), F32),
+            vmem((moves, 3, 2, 1, tall, LANES), F32),
             vmem((CYCLES + 1, nz, cx, ypad, LANES), F32),
             vmem((CYCLES + 1, nx * ny, cx, ypad, LANES), F32),
             vmem((7, nx * cx, ypad, LANES), F32),
-            vmem((2, nx * cx + 2, ypad + 2 * ROWS, LANES), F32),
+            vmem((3, nx * cx + 2, ypad + 2 * ROWS, LANES), F32),
             dma((2,)),
             dma((moves + 1, 26)),
             dma((moves + 1, 26)),

time: 48.2 us -> 55.8 us (1.16)
  Pallas kernels: 46.5 us -> 54.1 us
    pallas_call x1, Pallas kernels: 46.5 us -> 54.1 us  [body(): pl.pallas_call(functools.partial(kernel, counts, block), out_shape=jax.Sh...]
where the time goes in v3:
time: 55.8 us; the launch traced here: 55.7 us
  Pallas kernels  54.1 us (97%)
  local copies, waits for them, and re-layouts  1.57 us (3%)
    pallas_call x1, Pallas kernels, body(): pl.pallas_call(functools.partial(kernel, counts, block), out_shape=jax.Sh...  54.1 us
    unnamed x1, local copies, waits for them, and re-layouts  1.57 us

profile of v3, /device:TPU:0, one launch (start us, length us, event | category | flops | bytes accessed | tf_op | source)
XLA Modules:
  0.0 55.7 jit_solution(2837148270492353285)
XLA Ops:
  0.0 54.1 %shard_map.28 = f32[16,16,128]{2,1,0:T(8,128)} custom-call(f32[16,16,128]{2,1,0:T(8,128)} %s_ref.1, f32[16,16,128]{2,1,0:T(8,128)} %c_ref.1), custom_call_target="tpu_custom_call" | custom-call | tf_op jit(solution)/shard_map/pallas_call | solution.py:527
  54.1 1.6 %copy.4 = f32[16,16,128]{2,1,0:T(8,128)} copy(f32[16,16,128]{2,1,0:T(8,128)} %shard_map.28) | data formatting | bytes 262144

commit v4 on v3

--- a/solution.py
+++ b/solution.py
@@ -122,7 +122,11 @@
                 )
 
     spread[...] = jnp.zeros_like(spread)
-    for ref in (work_a, work_b, rim_a, rim_b):
+    work_a[...] = jnp.zeros_like(work_a)
+    for x in (0, px - 1):
+        work_b[x] = jnp.zeros(work_b.shape[1:], F32)
+    rim_a[...] = jnp.zeros_like(rim_a)
+    for ref in (work_b, rim_b):
         lead = ref.shape[:-2]
         ref[..., 0:ROWS, :] = jnp.zeros(lead + (ROWS, LANES), F32)
         ref[..., ROWS + py:, :] = jnp.zeros(lead + (ROWS, LANES), F32)
@@ -379,7 +383,6 @@
             coef[n, x] = w * faces[n]
         first = w * cs[1, x, body_rows]
         coef[6, x] = first
-        work_a[x, body_rows] = first
         scale[x] = (1.0 / OMEGA) * diag
     for slot, side in sides:
         c, near = near_rim(rim_c, tips, slot, side)
@@ -388,18 +391,46 @@
             rim_coef[n, slot, side] = w * faces[n]
         first = w * land_cs[slot, side, 1, body_rows]
         rim_coef[6, slot, side] = first
-        rim_a[slot, side, body_rows] = first
+
+    cc = gather_end(0)
+    shape = cc.shape
+    row = lax.broadcasted_iota(jnp.int32, shape, 1)
+    col = lax.broadcasted_iota(jnp.int32, shape, 2)
+    blank = jnp.zeros((1,) + shape[1:], F32)
+
+    def shifts(v):
+        return (
+            jnp.concatenate([blank, v[:-1]], axis=0),
+            jnp.concatenate([v[1:], blank], axis=0),
+            jnp.where(row == 0, 0.0, pltpu.roll(v, 1, 1)),
+            jnp.where(row == shape[1] - 1, 0.0, pltpu.roll(v, shape[1] - 1, 1)),
+            jnp.where(col == 0, 0.0, pltpu.roll(v, 1, 2)),
+            jnp.where(col == LANES - 1, 0.0, pltpu.roll(v, LANES - 1, 2)),
+        )
+
+    faces = [0.5 * (cc + n) for n in shifts(cc)]
+    diag = (faces[0] + faces[1]) + (faces[2] + faces[3]) + (faces[4] + faces[5])
+    here = cc > 0.0
+    w = jnp.where(here, OMEGA / jnp.where(here, diag, 1.0), 0.0)
+    for n in range(6):
+        coarse[n] = w * faces[n]
+    coarse[6] = w
+
+    sent(0, both, pack_cs, land_cs)
+    line_sent(0)
 
     field_a, field_b = (work_a, rim_a), (work_b, rim_b)
-    for cycle in range(CYCLES):
-        if cycle == 0:
-            order, first = [(field_a, field_b), (field_b, field_a), (field_a, field_b)], 2
-        else:
-            order = [(start, field_b), (field_b, field_a), (field_a, field_b), (field_b, field_a)]
-            first = 1
-        for i, (source, target) in enumerate(order):
-            sweep(source, target, first + i)
-        last = order[-1][1]
+
+    def sweeps():
+        def two(_, carry):
+            sweep(field_a, field_b, 1)
+            sweep(field_b, field_a, 1)
+            return carry
+        lax.fori_loop(0, SWEEPS // 2, two, 0)
+
+    def one_cycle(cycle, carry):
+        sweeps()
+        last = field_a
         which = 1 + 2 * cycle
         slot = which - 1
         main, packed, landed = fresh.at[slot], pack_v.at[slot], land_v.at[slot]
@@ -420,39 +451,9 @@
         gather_middle(1 + cycle)
 
         line_sent(1 + cycle)
-        if cycle == 0:
-            sent(0, both, pack_cs, land_cs)
-            line_sent(0)
-            plane_sent(0)
-        else:
-            plane_sent(cycle)
+        plane_sent(cycle)
         sent(which, main, packed, landed)
         arrive(which, main, packed, landed)
-
-        if cycle == 0:
-            cc = gather_end(0)
-            shape = cc.shape
-            row = lax.broadcasted_iota(jnp.int32, shape, 1)
-            col = lax.broadcasted_iota(jnp.int32, shape, 2)
-            blank = jnp.zeros((1,) + shape[1:], F32)
-
-            def shifts(v):
-                return (
-                    jnp.concatenate([blank, v[:-1]], axis=0),
-                    jnp.concatenate([v[1:], blank], axis=0),
-                    jnp.where(row == 0, 0.0, pltpu.roll(v, 1, 1)),
-                    jnp.where(row == shape[1] - 1, 0.0, pltpu.roll(v, shape[1] - 1, 1)),
-                    jnp.where(col == 0, 0.0, pltpu.roll(v, 1, 2)),
-                    jnp.where(col == LANES - 1, 0.0, pltpu.roll(v, LANES - 1, 2)),
-                )
-
-            faces = [0.5 * (cc + n) for n in shifts(cc)]
-            diag = (faces[0] + faces[1]) + (faces[2] + faces[3]) + (faces[4] + faces[5])
-            here = cc > 0.0
-            w = jnp.where(here, OMEGA / jnp.where(here, diag, 1.0), 0.0)
-            for n in range(6):
-                coarse[n] = w * faces[n]
-            coarse[6] = w
 
         rhs = gather_end(1 + cycle) * coarse[6]
         corr = rhs
@@ -491,24 +492,24 @@
             for k, lift in enumerate((lifted(1 + side, -1), own, lifted(1 + side, cx))):
                 rim_a[k, side, body_rows] = land_v[slot, k, side, 0, body_rows] + lift
 
-        sweep(field_a, field_b, 1)
-        sweep(field_b, field_a, 2)
-        sweep(field_a, field_b, 3)
-        ends = ends_of(rim_b, own_rows)
-        if cycle == CYCLES - 1:
-            for x in range(DEPTH, DEPTH + bx):
-                o_ref[x - DEPTH] = core(field_b, x, ends, 1.0 - OMEGA)
-        else:
-            which, slot = which + 1, slot + 1
-            main, packed, landed = fresh.at[slot], pack_v.at[slot], land_v.at[slot]
-            for x in range(DEPTH, DEPTH + bx):
-                fresh[slot, 0, x, 2 * ROWS:2 * ROWS + by] = core(field_b, x, ends, 1.0 - OMEGA)
-            send_flat(which, main, packed, landed)
-            send_deep(which, main, packed, landed)
-            sent(which, main, packed, landed)
-            arrive(which, main, packed, landed)
-            start = (fresh.at[slot, 0], land_v.at[slot, :, :, 0])
-
+        sweeps()
+
+        @pl.when(cycle < CYCLES - 1)
+        def _():
+            inner = (pl.ds(DEPTH, bx), own_rows)
+            main, packed, landed = fresh.at[slot + 1], pack_v.at[slot + 1], land_v.at[slot + 1]
+            fresh[slot + 1, 0, *inner] = work_a[inner]
+            send_flat(which + 1, main, packed, landed)
+            send_deep(which + 1, main, packed, landed)
+            sent(which + 1, main, packed, landed)
+            arrive(which + 1, main, packed, landed)
+            work_a[:, body_rows] = fresh[slot + 1, 0, :, body_rows]
+            for k, side in sides:
+                rim_a[k, side, body_rows] = land_v[slot + 1, k, side, 0, body_rows]
+
+        return carry
+    lax.fori_loop(0, CYCLES, one_cycle, 0)
+    o_ref[...] = work_a[pl.ds(DEPTH, bx), own_rows]
     plane_sent(CYCLES)
 
 

time: 55.8 us -> 68 us (1.22)
  Pallas kernels: 54.1 us -> 66.3 us
    pallas_call x1, Pallas kernels: 54.1 us -> 66.3 us  [body(): pl.pallas_call(functools.partial(kernel, counts, block), out_shape=jax.Sh...]
where the time goes in v4:
time: 68 us; the launch traced here: 67.8 us
  Pallas kernels  66.3 us (98%)
  local copies, waits for them, and re-layouts  1.57 us (2%)
    pallas_call x1, Pallas kernels, body(): pl.pallas_call(functools.partial(kernel, counts, block), out_shape=jax.Sh...  66.3 us
    unnamed x1, local copies, waits for them, and re-layouts  1.57 us

profile of v4, /device:TPU:0, one launch (start us, length us, event | category | flops | bytes accessed | tf_op | source)
XLA Modules:
  0.0 67.8 jit_solution(9710661476415635052)
XLA Ops:
  0.0 66.3 %shard_map.28 = f32[16,16,128]{2,1,0:T(8,128)} custom-call(f32[16,16,128]{2,1,0:T(8,128)} %s_ref.1, f32[16,16,128]{2,1,0:T(8,128)} %c_ref.1), custom_call_target="tpu_custom_call" | custom-call | tf_op jit(solution)/shard_map/pallas_call | solution.py:528
  66.3 1.6 %copy.4 = f32[16,16,128]{2,1,0:T(8,128)} copy(f32[16,16,128]{2,1,0:T(8,128)} %shard_map.28) | data formatting | bytes 262144

commit v5 on v2

--- a/solution.py
+++ b/solution.py
@@ -301,9 +301,11 @@
         return out
 
     def group_of(count):
-        return max(g for g in range(1, 12) if count % g == 0)
+        return max(g for g in range(1, 7) if count % g == 0)
 
     def sweep(source, target, margin):
+        if margin > 1 and group_of(px - 2 * margin) < 3:
+            margin = margin - 1
         count = px - 2 * margin
         size = group_of(count)
 

time: 48.2 us -> 49.5 us (1.027)
  Pallas kernels: 46.5 us -> 47.8 us
    pallas_call x1, Pallas kernels: 46.5 us -> 47.8 us  [body(): pl.pallas_call(functools.partial(kernel, counts, block), out_shape=jax.Sh...]
where the time goes in v5:
time: 49.5 us; the launch traced here: 49.4 us
  Pallas kernels  47.8 us (97%)
  local copies, waits for them, and re-layouts  1.57 us (3%)
    pallas_call x1, Pallas kernels, body(): pl.pallas_call(functools.partial(kernel, counts, block), out_shape=jax.Sh...  47.8 us
    unnamed x1, local copies, waits for them, and re-layouts  1.57 us

profile of v5, /device:TPU:0, one launch (start us, length us, event | category | flops | bytes accessed | tf_op | source)
XLA Modules:
  0.0 49.4 jit_solution(4508302411917814895)
XLA Ops:
  0.0 47.8 %shard_map.28 = f32[16,16,128]{2,1,0:T(8,128)} custom-call(f32[16,16,128]{2,1,0:T(8,128)} %s_ref.1, f32[16,16,128]{2,1,0:T(8,128)} %c_ref.1), custom_call_target="tpu_custom_call" | custom-call | tf_op jit(solution)/shard_map/pallas_call | solution.py:511
  47.8 1.6 %copy.4 = f32[16,16,128]{2,1,0:T(8,128)} copy(f32[16,16,128]{2,1,0:T(8,128)} %shard_map.28) | data formatting | bytes 262144
